TPU v7x, 32 devices: a whole 2x2x4 slice. The times are simulated.
32 devices in a mesh: row: 8 (over z, x), col: 4 (over y, core).
Axes of the slice: x: 2, y: 2, z: 4, core: 2. Of those that a mesh axis runs over, the one named last changes fastest.
Arguments:
- initial_heat: bfloat16 [48, 256, 1024], P(None, 'row', 'col'), may hold values from -6 to 6
- layer_conductance: bfloat16 [47, 256, 1024], P(None, 'row', 'col'), may hold values from 0.049804688 to 20
- layer_spacing: float32 [48], replicated, may hold values from 0.5 to 2
- submerged_layers: int32 [256, 1024], P('row', 'col'), may hold values from 1 to 48
- water_indicator: int32 [256, 1024], P('row', 'col'), may hold values from 0 to 1, as said below
- seafloor_distance: float32 [256, 1024], P('row', 'col'), may hold values from 0.5 to 2
Outputs:
- diffused_heat: float32 [48, 256, 1024], P(None, 'row', 'col')
- height: float32 [256, 1024], P('row', 'col')
Inputs may be any that keep to these rules, and one draw needn't show every extreme that they name: `water_indicator`: land lies in a few large regions and in scattered single cells.
All inputs are finite; a program needn't handle non-finite values.
Results may differ from a plain program's by a relative error of at most 0.0003.
Values sent between devices are 32-bit elements; how exact they have to be, the bound alone decides.
A program may use at most 64 MiB of HBM per device.

v0:
```python
import functools
import math

import jax
import jax.numpy as jnp
from jax import lax
from jax.experimental import pallas as pl
from jax.experimental.pallas import tpu as pltpu
from jax.sharding import PartitionSpec as P

ITERS = 4
SURFACE = 0.5
MESH = pl.DeviceIdType.MESH
GROUP = 4
SLOT = 8


def spread(field):
    rows, lanes = field.shape
    t = pltpu.roll(field, 1, 0) + pltpu.roll(field, rows - 1, 0)
    h = field + 0.5 * t
    return t + (pltpu.roll(h, 1, 1) + pltpu.roll(h, lanes - 1, 1))


def shift(block, by):
    lanes = block.shape[1]
    by = by % lanes
    return block if by == 0 else pltpu.roll(block, by, 1)


def kernel(
    n_row,
    n_col,
    heat_hbm,
    cond_hbm,
    spacing,
    wet_ref,
    water_ref,
    depth_ref,
    out_hbm,
    height_ref,
    heat,
    cond,
    ratios,
    values,
    ext,
    top_stage,
    bot_stage,
    west_stage,
    east_stage,
    land_n,
    land_s,
    land_w,
    land_e,
    land_c,
    col_max,
    row_max,
    in_sem,
    out_sem,
    send_sem,
    recv_sem,
    col_send,
    col_recv,
    row_send,
    row_recv,
):
    levels, rows, cols = heat.shape
    half = cols - 128
    row, col = lax.axis_index("row"), lax.axis_index("col")
    north, south = row > 0, row < n_row - 1
    up, down = lax.rem(row + n_row - 1, n_row), lax.rem(row + 1, n_row)
    west, east = lax.rem(col + n_col - 1, n_col), lax.rem(col + 1, n_col)

    get_heat = pltpu.make_async_copy(heat_hbm, heat, in_sem.at[0])
    get_cond = pltpu.make_async_copy(cond_hbm, cond, in_sem.at[1])
    get_heat.start()
    get_cond.start()

    barrier = pltpu.get_barrier_semaphore()

    def greet(r, c):
        pl.semaphore_signal(barrier, inc=1, device_id=(r, c), device_id_type=MESH)

    for off in range(1, n_col):
        greet(row, lax.rem(col + off, n_col))
    for off in range(1, n_row):
        greet(lax.rem(row + off, n_row), col)

    @pl.when(north)
    def _():
        greet(up, west)
        greet(up, east)

    @pl.when(south)
    def _():
        greet(down, west)
        greet(down, east)

    @pl.when(jnp.logical_not(north))
    def _():
        land_n[...] = jnp.zeros_like(land_n)
        land_c[0] = jnp.zeros_like(land_c[0])
        land_c[1] = jnp.zeros_like(land_c[1])

    @pl.when(jnp.logical_not(south))
    def _():
        land_s[...] = jnp.zeros_like(land_s)
        land_c[2] = jnp.zeros_like(land_c[2])
        land_c[3] = jnp.zeros_like(land_c[3])

    wet = wet_ref[...]
    mask = water_ref[...].astype(jnp.float32)
    masked_depth = mask * depth_ref[...]
    get_heat.wait()

    def add_levels(step, total):
        for j in range(GROUP):
            k = step * GROUP + j
            total = total + jnp.where(k < wet, spacing[k] * heat[k].astype(jnp.float32), 0.0)
        return total

    total = lax.fori_loop(0, levels // GROUP, add_levels, jnp.zeros((rows, cols), jnp.float32))
    forcing = mask * total / math.sqrt(levels)

    fields = (masked_depth, mask, forcing)
    for slot, field in enumerate(fields):
        ext[slot, :rows, :cols] = field
    sub8 = lax.broadcasted_iota(jnp.int32, (8, cols), 0)
    top_stage[0:8] = jnp.where(sub8 < 4, masked_depth[:8], pltpu.roll(mask[:8], 4, 0))
    top_stage[8:16] = forcing[:8]
    bot_stage[0:8] = jnp.where(sub8 >= 4, masked_depth[rows - 8 :], pltpu.roll(mask[rows - 8 :], 4, 0))
    bot_stage[8:16] = forcing[rows - 8 :]
    lane = lax.broadcasted_iota(jnp.int32, (rows, 128), 1)
    west_stage[...] = jnp.where(
        lane < SLOT,
        masked_depth[:, :128],
        jnp.where(lane < 2 * SLOT, shift(mask[:, :128], SLOT), shift(forcing[:, :128], 2 * SLOT)),
    )
    east_stage[...] = jnp.where(
        lane >= 128 - SLOT,
        masked_depth[:, half:],
        jnp.where(
            lane >= 128 - 2 * SLOT, shift(mask[:, half:], -SLOT), shift(forcing[:, half:], -2 * SLOT)
        ),
    )

    def remote(src, dst, slot, target):
        return pltpu.make_async_remote_copy(
            src_ref=src,
            dst_ref=dst,
            send_sem=send_sem.at[slot],
            recv_sem=recv_sem.at[slot],
            device_id=target,
            device_id_type=MESH,
        )

    low, high = pl.ds(0, 8), pl.ds(rows - 8, 8)
    to_n = remote(top_stage, land_s, 0, (up, col))
    to_s = remote(bot_stage, land_n, 1, (down, col))
    to_w = remote(west_stage, land_e, 2, (row, west))
    to_e = remote(east_stage, land_w, 3, (row, east))
    to_nw = remote(west_stage.at[low], land_c.at[3], 4, (up, west))
    to_ne = remote(east_stage.at[low], land_c.at[2], 5, (up, east))
    to_sw = remote(west_stage.at[high], land_c.at[1], 6, (down, west))
    to_se = remote(east_stage.at[high], land_c.at[0], 7, (down, east))
    northward, southward, sideways = (to_n, to_nw, to_ne), (to_s, to_sw, to_se), (to_w, to_e)

    diagonal = 2 * (north.astype(jnp.int32) + south.astype(jnp.int32))
    pl.semaphore_wait(barrier, n_row + n_col - 2 + diagonal)

    @pl.when(north)
    def _():
        for copy in northward:
            copy.start()

    @pl.when(south)
    def _():
        for copy in southward:
            copy.start()

    for copy in sideways:
        copy.start()

    get_cond.wait()

    def eliminate(k, carry):
        ratio, value, above, source, coupling = carry
        spread_out = spacing[k] + coupling + above * (1.0 - ratio)
        inverse = 1.0 / spread_out
        ratio = coupling * inverse
        value = (source + above * value) * inverse
        ratios[k] = ratio
        values[k] = value
        return ratio, value

    def forward(step, carry):
        ratio, value, above = carry
        for j in range(GROUP):
            k = step * GROUP + j
            coupling = jnp.where(k + 1 < wet, cond[k].astype(jnp.float32), 0.0)
            source = spacing[k] * heat[k].astype(jnp.float32)
            ratio, value = eliminate(k, (ratio, value, above, source, coupling))
            above = coupling
        return ratio, value, above

    zero = jnp.zeros((rows, cols), jnp.float32)
    whole = (levels - 1) // GROUP
    ratio, value, above = lax.fori_loop(0, whole, forward, (zero, zero, zero))
    for k in range(whole * GROUP, levels):
        source = spacing[k] * heat[k].astype(jnp.float32)
        if k < levels - 1:
            coupling = jnp.where(k + 1 < wet, cond[k].astype(jnp.float32), 0.0)
        else:
            coupling = zero
        ratio, value = eliminate(k, (ratio, value, above, source, coupling))
        above = coupling

    @pl.when(south)
    def _():
        for copy in northward:
            copy.wait_recv()

    @pl.when(north)
    def _():
        for copy in southward:
            copy.wait_recv()

    for copy in sideways:
        copy.wait_recv()

    from_n, from_s = land_n[...], land_s[...]
    ext[0, rows:, :cols] = jnp.where(sub8 < 4, from_s[:8], from_n[:8])
    ext[1, rows:, :cols] = pltpu.roll(jnp.where(sub8 >= 4, from_s[:8], from_n[:8]), 4, 0)
    ext[2, rows:, :cols] = jnp.where(sub8 < 4, from_s[8:], from_n[8:])
    sub_c = lax.broadcasted_iota(jnp.int32, (8, 128), 0)
    east_side = jnp.concatenate([land_e[...], jnp.where(sub_c < 4, land_c[3], land_c[1])], axis=0)
    west_side = jnp.concatenate([land_w[...], jnp.where(sub_c < 4, land_c[2], land_c[0])], axis=0)
    lane_x = lax.broadcasted_iota(jnp.int32, (rows + 8, 128), 1)
    for slot in range(3):
        ext[slot, :, cols:] = jnp.where(
            lane_x < 64, shift(east_side, -SLOT * slot), shift(west_side, SLOT * slot)
        )

    e, m = ext[0], ext[1]
    half_e, half_m = 0.5 * e, 0.5 * m
    centre = SURFACE + (half_e * spread(m) + half_m * spread(e))
    bound = 2.0 * centre[:rows, :cols] - SURFACE
    bound = jnp.max(bound, axis=0, keepdims=True)
    local = bound[:, :128]
    for start in range(128, cols, 128):
        local = jnp.maximum(local, bound[:, start : start + 128])
    col_max[0] = local

    def tell(buffer, off, sends, recvs, target):
        return pltpu.make_async_remote_copy(
            src_ref=buffer.at[0],
            dst_ref=buffer.at[off],
            send_sem=sends.at[off],
            recv_sem=recvs.at[off],
            device_id=target,
            device_id_type=MESH,
        )

    col_tells = [
        tell(col_max, off, col_send, col_recv, (row, lax.rem(col + off, n_col)))
        for off in range(1, n_col)
    ]
    row_tells = [
        tell(row_max, off, row_send, row_recv, (lax.rem(row + off, n_row), col))
        for off in range(1, n_row)
    ]
    for copy in col_tells:
        copy.start()

    parts = out_sem.shape[0]
    per = levels // parts

    def backward_part(part, carry):
        def backward(step, carry):
            for j in range(GROUP):
                k = (part + 1) * per - 1 - (step * GROUP + j)
                carry = values[k] + ratios[k] * carry
                values[k] = carry
            return carry

        carry = lax.fori_loop(0, per // GROUP, backward, carry)
        put = pltpu.make_async_copy(
            values.at[pl.ds(part * per, per)], out_hbm.at[pl.ds(part * per, per)], out_sem.at[part]
        )
        put.start()
        return carry, put

    carry = zero
    puts = []
    for part in reversed(range(parts // 2, parts)):
        carry, put = backward_part(part, carry)
        puts.append(put)

    for copy in col_tells:
        copy.wait_recv()
    best = col_max[0]
    for off in range(1, n_col):
        best = jnp.maximum(best, col_max[off])
    row_max[0] = best
    for copy in row_tells:
        copy.start()

    for part in reversed(range(parts // 2)):
        carry, put = backward_part(part, carry)
        puts.append(put)

    for copy in row_tells:
        copy.wait_recv()
    best = row_max[0]
    for off in range(1, n_row):
        best = jnp.maximum(best, row_max[off])
    top = jnp.max(best, axis=1, keepdims=True)

    theta = 0.5 * (top + SURFACE)
    delta = 0.5 * (top - SURFACE)
    sigma = theta / delta
    residual = ext[2]
    direction = residual * (1.0 / theta)
    recur = 1.0 / sigma
    result = jnp.zeros_like(residual)
    for _ in range(ITERS):
        result = result + direction
        image = centre * direction - (
            half_e * spread(m * direction) + half_m * spread(e * direction)
        )
        residual = residual - image
        recur_next = 1.0 / (2.0 * sigma - recur)
        direction = (recur_next * recur) * direction + (2.0 * recur_next / delta) * residual
        recur = recur_next
    height_ref[...] = (result + direction)[:rows, :cols]

    @pl.when(north)
    def _():
        for copy in northward:
            copy.wait_send()

    @pl.when(south)
    def _():
        for copy in southward:
            copy.wait_send()

    for copy in sideways + tuple(col_tells) + tuple(row_tells):
        copy.wait_send()
    for put in puts:
        put.wait()


def local(n_row, n_col, heat, cond, spacing, wet, water, depth):
    levels, rows, cols = heat.shape
    f32 = jnp.float32
    parts = 4
    vmem = pl.BlockSpec(memory_space=pltpu.VMEM)
    hbm = pl.BlockSpec(memory_space=pl.ANY)
    dma = pltpu.SemaphoreType.DMA
    return pl.pallas_call(
        functools.partial(kernel, n_row, n_col),
        out_shape=(
            jax.ShapeDtypeStruct((levels, rows, cols), f32),
            jax.ShapeDtypeStruct((rows, cols), f32),
        ),
        in_specs=[hbm, hbm, pl.BlockSpec(memory_space=pltpu.SMEM), vmem, vmem, vmem],
        out_specs=(hbm, vmem),
        scratch_shapes=[
            pltpu.VMEM((levels, rows, cols), heat.dtype),
            pltpu.VMEM((levels - 1, rows, cols), cond.dtype),
            pltpu.VMEM((levels, rows, cols), f32),
            pltpu.VMEM((levels, rows, cols), f32),
            pltpu.VMEM((3, rows + 8, cols + 128), f32),
            pltpu.VMEM((16, cols), f32),
            pltpu.VMEM((16, cols), f32),
            pltpu.VMEM((rows, 128), f32),
            pltpu.VMEM((rows, 128), f32),
            pltpu.VMEM((16, cols), f32),
            pltpu.VMEM((16, cols), f32),
            pltpu.VMEM((rows, 128), f32),
            pltpu.VMEM((rows, 128), f32),
            pltpu.VMEM((4, 8, 128), f32),
            pltpu.VMEM((n_col, 1, 128), f32),
            pltpu.VMEM((n_row, 1, 128), f32),
            dma((2,)),
            dma((parts,)),
            dma((8,)),
            dma((8,)),
            dma((n_col,)),
            dma((n_col,)),
            dma((n_row,)),
            dma((n_row,)),
        ],
        compiler_params=pltpu.CompilerParams(
            collective_id=0, has_side_effects=True, vmem_limit_bytes=32 * 1024 * 1024
        ),
    )(heat, cond, spacing, wet, water, depth)


def solution(mesh):
    placed = (
        P(None, "row", "col"),
        P(None, "row", "col"),
        P(),
        P("row", "col"),
        P("row", "col"),
        P("row", "col"),
    )
    return jax.shard_map(
        functools.partial(local, mesh.shape["row"], mesh.shape["col"]),
        mesh=mesh,
        in_specs=placed,
        out_specs=(P(None, "row", "col"), P("row", "col")),
        check_vma=False,
    )
```

profile of v0, /device:TPU:0, one launch (start us, length us, event | category | flops | bytes accessed | tf_op | source)
XLA Modules:
  0.0 24.9 jit_solution(3517850294241059839)
XLA Ops:
  0.6 0.0 copy-start
  0.6 1.1 %copy-done = bf16[48,32,256]{2,1,0:T(8,128)(2,1)S(1)} copy-done((bf16[48,32,256]{2,1,0:T(8,128)(2,1)S(1)}, bf16[48,32,256]{2,1,0:T(8,128)(2,1)}, u32[]{:S(2)}) %copy-start) | copy-done | bytes 786456
  1.8 0.0 copy-start.1
  1.8 1.1 %copy-done.1 = bf16[47,32,256]{2,1,0:T(8,128)(2,1)S(1)} copy-done((bf16[47,32,256]{2,1,0:T(8,128)(2,1)S(1)}, bf16[47,32,256]{2,1,0:T(8,128)(2,1)}, u32[]{:S(2)}) %copy-start.1) | copy-done | bytes 770072
  2.9 0.0 copy-start.2
  2.9 0.8 %copy-done.2 = s32[32,256]{1,0:T(8,128)S(1)} copy-done((s32[32,256]{1,0:T(8,128)S(1)}, s32[32,256]{1,0:T(8,128)}, u32[]{:S(2)}) %copy-start.2) | copy-done | bytes 32792
  3.7 0.0 copy-start.3
  3.7 0.8 %copy-done.3 = s32[32,256]{1,0:T(8,128)S(1)} copy-done((s32[32,256]{1,0:T(8,128)S(1)}, s32[32,256]{1,0:T(8,128)}, u32[]{:S(2)}) %copy-start.3) | copy-done | bytes 32792
  4.4 0.0 copy-start.4
  4.4 0.8 %copy-done.4 = f32[32,256]{1,0:T(8,128)S(1)} copy-done((f32[32,256]{1,0:T(8,128)S(1)}, f32[32,256]{1,0:T(8,128)}, u32[]{:S(2)}) %copy-start.4) | copy-done | bytes 32792
  5.2 0.0 copy-start.5
  5.2 0.7 %copy-done.5 = f32[48]{0:T(128)S(1)} copy-done((f32[48]{0:T(128)S(1)}, f32[48]{0:T(128)}, u32[]{:S(2)}) %copy-start.5) | copy-done | bytes 216
  5.8 17.3 %shard_map.77 = (f32[48,32,256]{2,1,0:T(8,128)S(1)}, f32[32,256]{1,0:T(8,128)S(1)}) custom-call(bf16[48,32,256]{2,1,0:T(8,128)(2,1)S(1)} %copy-done, bf16[47,32,256]{2,1,0:T(8,128)(2,1)S(1)} %copy-done.1, f32[48]{0:T(128)S(1)} %copy-done.5, s32[32,256]{1,0:T(8,128)S(1)} %copy-done.2, s32[32,256]{1,0:T(8,128)S(1)} %copy-done.3, f32[32,256]{1,0:T(8,128)S(1)} %copy-done.4), custom_call_target="tpu_custom_call" | custom-call | tf_op jit(solution)/shard_map/pallas_call | solution.py:360
  23.2 1.1 %copy.10 = f32[48,32,256]{2,1,0:T(8,128)} copy(f32[48,32,256]{2,1,0:T(8,128)S(1)} %get-tuple-element.4) | data formatting | bytes 3145728
  24.3 0.6 %copy.11 = f32[32,256]{1,0:T(8,128)} copy(f32[32,256]{1,0:T(8,128)S(1)} %get-tuple-element.5) | data formatting | bytes 65536
Async XLA Ops:
  0.6 1.1 %copy-start = (bf16[48,32,256]{2,1,0:T(8,128)(2,1)S(1)}, bf16[48,32,256]{2,1,0:T(8,128)(2,1)}, u32[]{:S(2)}) copy-start(bf16[48,32,256]{2,1,0:T(8,128)(2,1)} %heat_hbm.1) | copy-start | bytes 2359300
  1.8 1.1 %copy-start.1 = (bf16[47,32,256]{2,1,0:T(8,128)(2,1)S(1)}, bf16[47,32,256]{2,1,0:T(8,128)(2,1)}, u32[]{:S(2)}) copy-start(bf16[47,32,256]{2,1,0:T(8,128)(2,1)} %cond_hbm.1) | copy-start | bytes 2310148
  2.9 0.8 %copy-start.2 = (s32[32,256]{1,0:T(8,128)S(1)}, s32[32,256]{1,0:T(8,128)}, u32[]{:S(2)}) copy-start(s32[32,256]{1,0:T(8,128)} %wet_ref.1) | copy-start | bytes 98308
  3.7 0.8 %copy-start.3 = (s32[32,256]{1,0:T(8,128)S(1)}, s32[32,256]{1,0:T(8,128)}, u32[]{:S(2)}) copy-start(s32[32,256]{1,0:T(8,128)} %water_ref.1) | copy-start | bytes 98308
  4.4 0.8 %copy-start.4 = (f32[32,256]{1,0:T(8,128)S(1)}, f32[32,256]{1,0:T(8,128)}, u32[]{:S(2)}) copy-start(f32[32,256]{1,0:T(8,128)} %depth_ref.1) | copy-start | bytes 98308
  5.2 0.7 %copy-start.5 = (f32[48]{0:T(128)S(1)}, f32[48]{0:T(128)}, u32[]{:S(2)}) copy-start(f32[48]{0:T(128)} %spacing.1) | copy-start | bytes 580
where the time goes:
time: 25.3 us; the launch traced here: 24.9 us
  Pallas kernels  17.3 us (68%)
  local copies, waits for them, and re-layouts  6.94 us (27%)
  between operations  0.65 us (3%)
    pallas_call x1, Pallas kernels, local(): pl.pallas_call(functools.partial(kernel, n_row, n_col), out_shape=(jax.Sh...  17.3 us
    unnamed x14, local copies, waits for them, and re-layouts  6.94 us

commit v1 on v0

--- a/solution.py
+++ b/solution.py
@@ -12,6 +12,7 @@
 SURFACE = 0.5
 MESH = pl.DeviceIdType.MESH
 GROUP = 4
+GRANT = 60 * 1024 * 1024
 SLOT = 8
 
 
@@ -33,16 +34,21 @@
     n_col,
     heat_hbm,
     cond_hbm,
+    spacing_hbm,
+    wet_hbm,
+    water_hbm,
+    depth_hbm,
+    out_hbm,
+    height_hbm,
+    heat,
+    cond,
     spacing,
     wet_ref,
     water_ref,
     depth_ref,
-    out_hbm,
-    height_ref,
-    heat,
-    cond,
     ratios,
     values,
+    height_ref,
     ext,
     top_stage,
     bot_stage,
@@ -71,10 +77,18 @@
     up, down = lax.rem(row + n_row - 1, n_row), lax.rem(row + 1, n_row)
     west, east = lax.rem(col + n_col - 1, n_col), lax.rem(col + 1, n_col)
 
-    get_heat = pltpu.make_async_copy(heat_hbm, heat, in_sem.at[0])
-    get_cond = pltpu.make_async_copy(cond_hbm, cond, in_sem.at[1])
-    get_heat.start()
-    get_cond.start()
+    pairs = (
+        (wet_hbm, wet_ref),
+        (spacing_hbm, spacing),
+        (water_hbm, water_ref),
+        (depth_hbm, depth_ref),
+        (heat_hbm, heat),
+        (cond_hbm, cond),
+    )
+    gets = [pltpu.make_async_copy(a, b, in_sem.at[i]) for i, (a, b) in enumerate(pairs)]
+    for get in gets:
+        get.start()
+    get_cond = gets.pop()
 
     barrier = pltpu.get_barrier_semaphore()
 
@@ -108,10 +122,11 @@
         land_c[2] = jnp.zeros_like(land_c[2])
         land_c[3] = jnp.zeros_like(land_c[3])
 
+    for get in gets:
+        get.wait()
     wet = wet_ref[...]
     mask = water_ref[...].astype(jnp.float32)
     masked_depth = mask * depth_ref[...]
-    get_heat.wait()
 
     def add_levels(step, total):
         for j in range(GROUP):
@@ -272,7 +287,7 @@
     for copy in col_tells:
         copy.start()
 
-    parts = out_sem.shape[0]
+    parts = out_sem.shape[0] - 1
     per = levels // parts
 
     def backward_part(part, carry):
@@ -284,9 +299,8 @@
             return carry
 
         carry = lax.fori_loop(0, per // GROUP, backward, carry)
-        put = pltpu.make_async_copy(
-            values.at[pl.ds(part * per, per)], out_hbm.at[pl.ds(part * per, per)], out_sem.at[part]
-        )
+        span = pl.ds(part * per, per)
+        put = pltpu.make_async_copy(values.at[span], out_hbm.at[span], out_sem.at[part])
         put.start()
         return carry, put
 
@@ -333,6 +347,9 @@
         direction = (recur_next * recur) * direction + (2.0 * recur_next / delta) * residual
         recur = recur_next
     height_ref[...] = (result + direction)[:rows, :cols]
+    put = pltpu.make_async_copy(height_ref, height_hbm, out_sem.at[parts])
+    put.start()
+    puts.append(put)
 
     @pl.when(north)
     def _():
@@ -350,26 +367,43 @@
         put.wait()
 
 
+def store(heat, height, heat_out, height_out, sem):
+    parts = sem.shape[0] - 1
+    per = heat.shape[0] // parts
+    puts = [pltpu.make_async_copy(height, height_out, sem.at[parts])]
+    for part in range(parts):
+        span = pl.ds(part * per, per)
+        puts.append(pltpu.make_async_copy(heat.at[span], heat_out.at[span], sem.at[part]))
+    for put in puts:
+        put.start()
+    for put in puts:
+        put.wait()
+
+
 def local(n_row, n_col, heat, cond, spacing, wet, water, depth):
     levels, rows, cols = heat.shape
     f32 = jnp.float32
-    parts = 4
-    vmem = pl.BlockSpec(memory_space=pltpu.VMEM)
-    hbm = pl.BlockSpec(memory_space=pl.ANY)
+    hbm = pl.BlockSpec(memory_space=pltpu.HBM)
     dma = pltpu.SemaphoreType.DMA
-    return pl.pallas_call(
+    shapes = (
+        jax.ShapeDtypeStruct((levels, rows, cols), f32),
+        jax.ShapeDtypeStruct((rows, cols), f32),
+    )
+    mixed, height = pl.pallas_call(
         functools.partial(kernel, n_row, n_col),
-        out_shape=(
-            jax.ShapeDtypeStruct((levels, rows, cols), f32),
-            jax.ShapeDtypeStruct((rows, cols), f32),
-        ),
-        in_specs=[hbm, hbm, pl.BlockSpec(memory_space=pltpu.SMEM), vmem, vmem, vmem],
-        out_specs=(hbm, vmem),
+        out_shape=shapes,
+        in_specs=[hbm] * 6,
+        out_specs=(hbm, hbm),
         scratch_shapes=[
             pltpu.VMEM((levels, rows, cols), heat.dtype),
             pltpu.VMEM((levels - 1, rows, cols), cond.dtype),
+            pltpu.SMEM((levels,), f32),
+            pltpu.VMEM((rows, cols), wet.dtype),
+            pltpu.VMEM((rows, cols), water.dtype),
+            pltpu.VMEM((rows, cols), f32),
             pltpu.VMEM((levels, rows, cols), f32),
             pltpu.VMEM((levels, rows, cols), f32),
+            pltpu.VMEM((rows, cols), f32),
             pltpu.VMEM((3, rows + 8, cols + 128), f32),
             pltpu.VMEM((16, cols), f32),
             pltpu.VMEM((16, cols), f32),
@@ -382,8 +416,8 @@
             pltpu.VMEM((4, 8, 128), f32),
             pltpu.VMEM((n_col, 1, 128), f32),
             pltpu.VMEM((n_row, 1, 128), f32),
-            dma((2,)),
-            dma((parts,)),
+            dma((6,)),
+            dma((5,)),
             dma((8,)),
             dma((8,)),
             dma((n_col,)),
@@ -392,9 +426,17 @@
             dma((n_row,)),
         ],
         compiler_params=pltpu.CompilerParams(
-            collective_id=0, has_side_effects=True, vmem_limit_bytes=32 * 1024 * 1024
+            collective_id=0, has_side_effects=True, vmem_limit_bytes=GRANT
         ),
     )(heat, cond, spacing, wet, water, depth)
+    return pl.pallas_call(
+        store,
+        out_shape=shapes,
+        in_specs=[hbm, hbm],
+        out_specs=(hbm, hbm),
+        scratch_shapes=[dma((5,))],
+        compiler_params=pltpu.CompilerParams(has_side_effects=True, vmem_limit_bytes=GRANT),
+    )(mixed, height)
 
 
 def solution(mesh):

time: 25.3 us -> 67.6 us (2.67)
  Pallas kernels: 17.3 us -> 66.8 us
  local copies, waits for them, and re-layouts: 6.94 us -> 0 us
    pallas_call x1 -> x2, Pallas kernels: 17.3 us -> 66.8 us  [the longest x1 49.8 us: local(): pl.pallas_call(store, out_shape=shapes, in_specs=[hbm, hbm], out_specs=(h...]
    unnamed x14 -> x0, local copies, waits for them, and re-layouts: 6.94 us -> none
where the time goes in v1:
time: 67.6 us; the launch traced here: 67.5 us
  Pallas kernels  66.8 us (99%)
    pallas_call x1, Pallas kernels, local(): pl.pallas_call(store, out_shape=shapes, in_specs=[hbm, hbm], out_specs=(h...  49.8 us
    pallas_call x1, Pallas kernels, local(): pl.pallas_call(functools.partial(kernel, n_row, n_col), out_shape=shapes,...  17 us

profile of v1, /device:TPU:0, one launch (start us, length us, event | category | flops | bytes accessed | tf_op | source)
XLA Modules:
  0.0 67.5 jit_solution(10004673173161245463)
XLA Ops:
  0.6 17.0 %shard_map.77 = (f32[48,32,256]{2,1,0:T(8,128)}, f32[32,256]{1,0:T(8,128)}) custom-call(bf16[48,32,256]{2,1,0:T(8,128)(2,1)} %heat_hbm.1, bf16[47,32,256]{2,1,0:T(8,128)(2,1)} %cond_hbm.1, f32[48]{0:T(128)} %spacing_hbm.1, s32[32,256]{1,0:T(8,128)} %wet_hbm.1, s32[32,256]{1,0:T(8,128)} %water_hbm.1, f32[32,256]{1,0:T(8,128)} %depth_hbm.1), custom_call_target="tpu_custom_call" | custom-call | tf_op jit(solution)/shard_map/pallas_call | solution.py:392
  17.7 49.8 %shard_map.78 = (f32[48,32,256]{2,1,0:T(8,128)}, f32[32,256]{1,0:T(8,128)}) custom-call(f32[48,32,256]{2,1,0:T(8,128)} %get-tuple-element.4.heat, f32[32,256]{1,0:T(8,128)} %get-tuple-element.5.height), custom_call_target="tpu_custom_call" | custom-call | tf_op jit(solution)/shard_map/pallas_call | solution.py:432

commit v2 on v1

--- a/solution.py
+++ b/solution.py
@@ -12,7 +12,7 @@
 SURFACE = 0.5
 MESH = pl.DeviceIdType.MESH
 GROUP = 4
-GRANT = 60 * 1024 * 1024
+GRANT = 32 * 1024 * 1024
 SLOT = 8
 
 
@@ -38,8 +38,8 @@
     wet_hbm,
     water_hbm,
     depth_hbm,
-    out_hbm,
-    height_hbm,
+    values,
+    height_ref,
     heat,
     cond,
     spacing,
@@ -47,8 +47,6 @@
     water_ref,
     depth_ref,
     ratios,
-    values,
-    height_ref,
     ext,
     top_stage,
     bot_stage,
@@ -62,7 +60,6 @@
     col_max,
     row_max,
     in_sem,
-    out_sem,
     send_sem,
     recv_sem,
     col_send,
@@ -287,7 +284,7 @@
     for copy in col_tells:
         copy.start()
 
-    parts = out_sem.shape[0] - 1
+    parts = 2
     per = levels // parts
 
     def backward_part(part, carry):
@@ -298,17 +295,9 @@
                 values[k] = carry
             return carry
 
-        carry = lax.fori_loop(0, per // GROUP, backward, carry)
-        span = pl.ds(part * per, per)
-        put = pltpu.make_async_copy(values.at[span], out_hbm.at[span], out_sem.at[part])
-        put.start()
-        return carry, put
-
-    carry = zero
-    puts = []
-    for part in reversed(range(parts // 2, parts)):
-        carry, put = backward_part(part, carry)
-        puts.append(put)
+        return lax.fori_loop(0, per // GROUP, backward, carry)
+
+    carry = backward_part(1, zero)
 
     for copy in col_tells:
         copy.wait_recv()
@@ -319,9 +308,7 @@
     for copy in row_tells:
         copy.start()
 
-    for part in reversed(range(parts // 2)):
-        carry, put = backward_part(part, carry)
-        puts.append(put)
+    backward_part(0, carry)
 
     for copy in row_tells:
         copy.wait_recv()
@@ -347,9 +334,6 @@
         direction = (recur_next * recur) * direction + (2.0 * recur_next / delta) * residual
         recur = recur_next
     height_ref[...] = (result + direction)[:rows, :cols]
-    put = pltpu.make_async_copy(height_ref, height_hbm, out_sem.at[parts])
-    put.start()
-    puts.append(put)
 
     @pl.when(north)
     def _():
@@ -363,8 +347,6 @@
 
     for copy in sideways + tuple(col_tells) + tuple(row_tells):
         copy.wait_send()
-    for put in puts:
-        put.wait()
 
 
 def store(heat, height, heat_out, height_out, sem):
@@ -383,17 +365,22 @@
 def local(n_row, n_col, heat, cond, spacing, wet, water, depth):
     levels, rows, cols = heat.shape
     f32 = jnp.float32
+    vmem = pl.BlockSpec(memory_space=pltpu.VMEM)
     hbm = pl.BlockSpec(memory_space=pltpu.HBM)
     dma = pltpu.SemaphoreType.DMA
     shapes = (
         jax.ShapeDtypeStruct((levels, rows, cols), f32),
         jax.ShapeDtypeStruct((rows, cols), f32),
     )
+    held = [
+        pltpu.with_memory_space_constraint(x, pltpu.HBM)
+        for x in (heat, cond, spacing, wet, water, depth)
+    ]
     mixed, height = pl.pallas_call(
         functools.partial(kernel, n_row, n_col),
         out_shape=shapes,
         in_specs=[hbm] * 6,
-        out_specs=(hbm, hbm),
+        out_specs=(vmem, vmem),
         scratch_shapes=[
             pltpu.VMEM((levels, rows, cols), heat.dtype),
             pltpu.VMEM((levels - 1, rows, cols), cond.dtype),
@@ -402,8 +389,6 @@
             pltpu.VMEM((rows, cols), water.dtype),
             pltpu.VMEM((rows, cols), f32),
             pltpu.VMEM((levels, rows, cols), f32),
-            pltpu.VMEM((levels, rows, cols), f32),
-            pltpu.VMEM((rows, cols), f32),
             pltpu.VMEM((3, rows + 8, cols + 128), f32),
             pltpu.VMEM((16, cols), f32),
             pltpu.VMEM((16, cols), f32),
@@ -417,7 +402,6 @@
             pltpu.VMEM((n_col, 1, 128), f32),
             pltpu.VMEM((n_row, 1, 128), f32),
             dma((6,)),
-            dma((5,)),
             dma((8,)),
             dma((8,)),
             dma((n_col,)),
@@ -428,11 +412,11 @@
         compiler_params=pltpu.CompilerParams(
             collective_id=0, has_side_effects=True, vmem_limit_bytes=GRANT
         ),
-    )(heat, cond, spacing, wet, water, depth)
+    )(*held)
     return pl.pallas_call(
         store,
         out_shape=shapes,
-        in_specs=[hbm, hbm],
+        in_specs=[vmem, vmem],
         out_specs=(hbm, hbm),
         scratch_shapes=[dma((5,))],
         compiler_params=pltpu.CompilerParams(has_side_effects=True, vmem_limit_bytes=GRANT),

time: 67.6 us -> 18.4 us (0.27)
  Pallas kernels: 66.8 us -> 17.6 us
    pallas_call x1, Pallas kernels: 49.8 us -> 1.19 us  [local(): pl.pallas_call(store, out_shape=shapes, in_specs=[vmem, vmem], out_specs=...]
where the time goes in v2:
time: 18.4 us; the launch traced here: 18.2 us
  Pallas kernels  17.6 us (96%)
  between operations  0.64 us (3%)
    pallas_call x1, Pallas kernels, local(): pl.pallas_call(functools.partial(kernel, n_row, n_col), out_shape=shapes,...  16.4 us
    pallas_call x1, Pallas kernels, local(): pl.pallas_call(store, out_shape=shapes, in_specs=[vmem, vmem], out_specs=...  1.19 us

profile of v2, /device:TPU:0, one launch (start us, length us, event | category | flops | bytes accessed | tf_op | source)
XLA Modules:
  0.0 18.2 jit_solution(17014378241164912052)
XLA Ops:
  0.6 16.4 %shard_map.77 = (f32[48,32,256]{2,1,0:T(8,128)S(1)}, f32[32,256]{1,0:T(8,128)S(1)}) custom-call(bf16[48,32,256]{2,1,0:T(8,128)(2,1)} %heat_hbm.1, bf16[47,32,256]{2,1,0:T(8,128)(2,1)} %cond_hbm.1, f32[48]{0:T(128)} %spacing_hbm.1, s32[32,256]{1,0:T(8,128)} %wet_hbm.1, s32[32,256]{1,0:T(8,128)} %water_hbm.1, f32[32,256]{1,0:T(8,128)} %depth_hbm.1), custom_call_target="tpu_custom_call" | custom-call | tf_op jit(solution)/shard_map/pallas_call | solution.py:379
  17.0 1.2 %shard_map.78 = (f32[48,32,256]{2,1,0:T(8,128)}, f32[32,256]{1,0:T(8,128)}) custom-call(f32[48,32,256]{2,1,0:T(8,128)S(1)} %get-tuple-element.4.heat, f32[32,256]{1,0:T(8,128)S(1)} %get-tuple-element.5.height), custom_call_target="tpu_custom_call" | custom-call | tf_op jit(solution)/shard_map/pallas_call | solution.py:416

commit v3 on v2

v3 whole, which is shorter than its diff:
```python
import functools
import math

import jax
import jax.numpy as jnp
from jax import lax
from jax.experimental import pallas as pl
from jax.experimental.pallas import tpu as pltpu
from jax.sharding import PartitionSpec as P

ITERS = 4
SURFACE = 0.5
MESH = pl.DeviceIdType.MESH
GROUP = 4
GRANT = 32 * 1024 * 1024
SLOT = 8


def spread(field):
    rows, lanes = field.shape
    t = pltpu.roll(field, 1, 0) + pltpu.roll(field, rows - 1, 0)
    h = field + 0.5 * t
    return t + (pltpu.roll(h, 1, 1) + pltpu.roll(h, lanes - 1, 1))


def shift(block, by):
    lanes = block.shape[1]
    by = by % lanes
    return block if by == 0 else pltpu.roll(block, by, 1)


def pack_west(blocks):
    lane = lax.broadcasted_iota(jnp.int32, blocks[0].shape, 1)
    out = blocks[0]
    for slot in range(1, len(blocks)):
        out = jnp.where(lane >= SLOT * slot, shift(blocks[slot], SLOT * slot), out)
    return out


def pack_east(blocks):
    lane = lax.broadcasted_iota(jnp.int32, blocks[0].shape, 1)
    out = blocks[0]
    for slot in range(1, len(blocks)):
        out = jnp.where(lane < 128 - SLOT * slot, shift(blocks[slot], -SLOT * slot), out)
    return out


def kernel(
    n_row,
    n_col,
    heat_hbm,
    cond_hbm,
    spacing_hbm,
    wet_hbm,
    water_hbm,
    depth_hbm,
    ratios,
    values,
    height_ref,
    heat,
    cond,
    spacing,
    wet_ref,
    water_ref,
    depth_ref,
    ext,
    edge,
    side,
    land_edge,
    land_side,
    col_max,
    row_max,
    in_sem,
    send_sem,
    recv_sem,
    col_send,
    col_recv,
    row_send,
    row_recv,
):
    levels, rows, cols = heat.shape
    half = cols - 128
    tiles = rows // 8
    row, col = lax.axis_index("row"), lax.axis_index("col")
    north, south = row > 0, row < n_row - 1
    up, down = lax.rem(row + n_row - 1, n_row), lax.rem(row + 1, n_row)
    west, east = lax.rem(col + n_col - 1, n_col), lax.rem(col + 1, n_col)

    pairs = (
        (water_hbm, water_ref),
        (depth_hbm, depth_ref),
        (wet_hbm, wet_ref),
        (spacing_hbm, spacing),
        (heat_hbm, heat),
        (cond_hbm, cond),
    )
    gets = [pltpu.make_async_copy(a, b, in_sem.at[i]) for i, (a, b) in enumerate(pairs)]
    for get in gets:
        get.start()

    barrier = pltpu.get_barrier_semaphore()

    def greet(r, c):
        pl.semaphore_signal(barrier, inc=1, device_id=(r, c), device_id_type=MESH)

    for off in range(1, n_col):
        greet(row, lax.rem(col + off, n_col))
    for off in range(1, n_row):
        greet(lax.rem(row + off, n_row), col)

    @pl.when(north)
    def _():
        greet(up, west)
        greet(up, east)

    @pl.when(south)
    def _():
        greet(down, west)
        greet(down, east)

    @pl.when(jnp.logical_not(north))
    def _():
        for kind in range(2):
            for place in (2, 3):
                land_side[kind, place] = jnp.zeros((8, 128), jnp.float32)
            land_edge[kind, 0] = jnp.zeros((8, cols), jnp.float32)

    @pl.when(jnp.logical_not(south))
    def _():
        for kind in range(2):
            for place in (4, 5):
                land_side[kind, place] = jnp.zeros((8, 128), jnp.float32)
            land_edge[kind, 1] = jnp.zeros((8, cols), jnp.float32)

    def halo_copies(kind):
        def remote(src, dst, slot, target):
            return pltpu.make_async_remote_copy(
                src_ref=src,
                dst_ref=dst,
                send_sem=send_sem.at[kind, slot],
                recv_sem=recv_sem.at[kind, slot],
                device_id=target,
                device_id_type=MESH,
            )

        from_west, from_east = side.at[kind, 0], side.at[kind, 1]
        northward = (
            remote(edge.at[kind, 0], land_edge.at[kind, 1], 0, (up, col)),
            remote(from_west, land_side.at[kind, 5], 1, (up, west)),
            remote(from_east, land_side.at[kind, 4], 2, (up, east)),
        )
        southward = (
            remote(edge.at[kind, 1], land_edge.at[kind, 0], 3, (down, col)),
            remote(from_west, land_side.at[kind, 3], 4, (down, west)),
            remote(from_east, land_side.at[kind, 2], 5, (down, east)),
        )
        sideways = (
            remote(from_west, land_side.at[kind, 1], 6, (row, west)),
            remote(from_east, land_side.at[kind, 0], 7, (row, east)),
        )
        return northward, southward, sideways

    def start_halo(kind):
        northward, southward, sideways = halo_copies(kind)

        @pl.when(north)
        def _():
            for copy in northward:
                copy.start()

        @pl.when(south)
        def _():
            for copy in southward:
                copy.start()

        for copy in sideways:
            copy.start()

    def wait_halo(kind):
        northward, southward, sideways = halo_copies(kind)

        @pl.when(south)
        def _():
            for copy in northward:
                copy.wait_recv()

        @pl.when(north)
        def _():
            for copy in southward:
                copy.wait_recv()

        for copy in sideways:
            copy.wait_recv()

    def end_halo(kind):
        northward, southward, sideways = halo_copies(kind)

        @pl.when(north)
        def _():
            for copy in northward:
                copy.wait_send()

        @pl.when(south)
        def _():
            for copy in southward:
                copy.wait_send()

        for copy in sideways:
            copy.wait_send()

    def stage_sides(kind, fields):
        blocks = [f[8 * t : 8 * t + 8, :128] for f in fields for t in range(tiles)]
        side[kind, 0] = pack_west(blocks)
        blocks = [f[8 * t : 8 * t + 8, half:] for f in fields for t in range(tiles)]
        side[kind, 1] = pack_east(blocks)

    sub_c = lax.broadcasted_iota(jnp.int32, (8, 128), 0)
    lane_c = lax.broadcasted_iota(jnp.int32, (8, 128), 1)

    def widen_sides(kind, slot, target):
        w, e, nw, ne, sw, se = (land_side[kind, place] for place in range(6))
        for t in range(tiles):
            by = SLOT * (slot * tiles + t)
            ext[target, pl.ds(8 * t, 8), cols:] = jnp.where(lane_c < 64, shift(e, -by), shift(w, by))
        first, last = SLOT * slot * tiles, SLOT * (slot * tiles + tiles - 1)
        above = jnp.where(lane_c < 64, shift(ne, -last), shift(nw, last))
        below = jnp.where(lane_c < 64, shift(se, -first), shift(sw, first))
        ext[target, rows:, cols:] = jnp.where(sub_c < 4, below, above)

    gets[0].wait()
    gets[1].wait()
    mask = water_ref[...].astype(jnp.float32)
    masked_depth = mask * depth_ref[...]
    ext[0, :rows, :cols] = masked_depth
    ext[1, :rows, :cols] = mask
    sub8 = lax.broadcasted_iota(jnp.int32, (8, cols), 0)
    edge[0, 0] = jnp.where(sub8 < 4, masked_depth[:8], pltpu.roll(mask[:8], 4, 0))
    edge[0, 1] = jnp.where(sub8 >= 4, masked_depth[rows - 8 :], pltpu.roll(mask[rows - 8 :], 4, 0))
    stage_sides(0, (masked_depth, mask))

    diagonal = 2 * (north.astype(jnp.int32) + south.astype(jnp.int32))
    pl.semaphore_wait(barrier, n_row + n_col - 2 + diagonal)
    start_halo(0)

    for get in gets[2:5]:
        get.wait()
    wet = wet_ref[...]

    def add_levels(step, total):
        for j in range(GROUP):
            k = step * GROUP + j
            total = total + jnp.where(k < wet, spacing[k] * heat[k].astype(jnp.float32), 0.0)
        return total

    zero = jnp.zeros((rows, cols), jnp.float32)
    total = lax.fori_loop(0, levels // GROUP, add_levels, zero)
    forcing = mask * total / math.sqrt(levels)
    ext[2, :rows, :cols] = forcing
    edge[1, 0] = forcing[:8]
    edge[1, 1] = forcing[rows - 8 :]
    stage_sides(1, (forcing,))
    start_halo(1)

    wait_halo(0)
    from_n, from_s = land_edge[0, 0], land_edge[0, 1]
    ext[0, rows:, :cols] = jnp.where(sub8 < 4, from_s, from_n)
    ext[1, rows:, :cols] = pltpu.roll(jnp.where(sub8 >= 4, from_s, from_n), 4, 0)
    widen_sides(0, 0, 0)
    widen_sides(0, 1, 1)
    e, m = ext[0], ext[1]
    half_e, half_m = 0.5 * e, 0.5 * m
    centre = SURFACE + (half_e * spread(m) + half_m * spread(e))
    ext[3] = centre
    bound = jnp.max(2.0 * centre[:rows, :cols] - SURFACE, axis=0, keepdims=True)
    local = bound[:, :128]
    for start in range(128, cols, 128):
        local = jnp.maximum(local, bound[:, start : start + 128])
    col_max[0] = local

    def tell(buffer, off, sends, recvs, target):
        return pltpu.make_async_remote_copy(
            src_ref=buffer.at[0],
            dst_ref=buffer.at[off],
            send_sem=sends.at[off],
            recv_sem=recvs.at[off],
            device_id=target,
            device_id_type=MESH,
        )

    col_tells = [
        tell(col_max, off, col_send, col_recv, (row, lax.rem(col + off, n_col)))
        for off in range(1, n_col)
    ]
    row_tells = [
        tell(row_max, off, row_send, row_recv, (lax.rem(row + off, n_row), col))
        for off in range(1, n_row)
    ]
    for copy in col_tells:
        copy.start()

    gets[5].wait()

    def eliminate(k, carry, coupling):
        ratio, value, above = carry
        inverse = 1.0 / (spacing[k] + coupling + above * (1.0 - ratio))
        source = spacing[k] * heat[k].astype(jnp.float32)
        ratio = coupling * inverse
        value = (source + above * value) * inverse
        ratios[k] = ratio
        values[k] = value
        return ratio, value, coupling

    def forward(step, carry):
        for j in range(GROUP):
            k = step * GROUP + j
            coupling = jnp.where(k + 1 < wet_ref[...], cond[k].astype(jnp.float32), 0.0)
            carry = eliminate(k, carry, coupling)
        return carry

    steps = (levels - 1) // GROUP
    carry = lax.fori_loop(0, steps // 2, forward, (zero, zero, zero))

    for copy in col_tells:
        copy.wait_recv()
    best = col_max[0]
    for off in range(1, n_col):
        best = jnp.maximum(best, col_max[off])
    row_max[0] = best
    for copy in row_tells:
        copy.start()

    carry = lax.fori_loop(steps // 2, steps, forward, carry)
    for k in range(steps * GROUP, levels):
        coupling = zero
        if k < levels - 1:
            coupling = jnp.where(k + 1 < wet_ref[...], cond[k].astype(jnp.float32), 0.0)
        carry = eliminate(k, carry, coupling)

    wait_halo(1)
    ext[2, rows:, :cols] = jnp.where(sub8 < 4, land_edge[1, 1], land_edge[1, 0])
    widen_sides(1, 0, 2)

    for copy in row_tells:
        copy.wait_recv()
    best = row_max[0]
    for off in range(1, n_row):
        best = jnp.maximum(best, row_max[off])
    top = jnp.max(best, axis=1, keepdims=True)

    theta = 0.5 * (top + SURFACE)
    delta = 0.5 * (top - SURFACE)
    sigma = theta / delta
    e, m, residual, centre = ext[0], ext[1], ext[2], ext[3]
    half_e, half_m = 0.5 * e, 0.5 * m
    direction = residual * (1.0 / theta)
    recur = 1.0 / sigma
    result = jnp.zeros_like(residual)
    for _ in range(ITERS):
        result = result + direction
        image = centre * direction - (
            half_e * spread(m * direction) + half_m * spread(e * direction)
        )
        residual = residual - image
        recur_next = 1.0 / (2.0 * sigma - recur)
        direction = (recur_next * recur) * direction + (2.0 * recur_next / delta) * residual
        recur = recur_next
    height_ref[...] = (result + direction)[:rows, :cols]

    end_halo(0)
    end_halo(1)
    for copy in col_tells + row_tells:
        copy.wait_send()


def finish(ratios, values, height, heat_out, height_out, heat, sem):
    levels, rows, cols = values.shape
    parts = sem.shape[0] - 1
    per = levels // parts
    puts = [pltpu.make_async_copy(height, height_out, sem.at[parts])]
    puts[0].start()
    carry = jnp.zeros((rows, cols), jnp.float32)
    for part in reversed(range(parts)):
        for k in reversed(range(part * per, (part + 1) * per)):
            carry = values[k] + ratios[k] * carry
            heat[k] = carry
        span = pl.ds(part * per, per)
        puts.append(pltpu.make_async_copy(heat.at[span], heat_out.at[span], sem.at[part]))
        puts[-1].start()
    for put in puts:
        put.wait()


def local(n_row, n_col, heat, cond, spacing, wet, water, depth):
    levels, rows, cols = heat.shape
    f32 = jnp.float32
    parts = 6
    vmem = pl.BlockSpec(memory_space=pltpu.VMEM)
    hbm = pl.BlockSpec(memory_space=pltpu.HBM)
    dma = pltpu.SemaphoreType.DMA
    column = jax.ShapeDtypeStruct((levels, rows, cols), f32)
    surface = jax.ShapeDtypeStruct((rows, cols), f32)
    held = [
        pltpu.with_memory_space_constraint(x, pltpu.HBM)
        for x in (heat, cond, spacing, wet, water, depth)
    ]
    ratios, values, height = pl.pallas_call(
        functools.partial(kernel, n_row, n_col),
        out_shape=(column, column, surface),
        in_specs=[hbm] * 6,
        out_specs=(vmem, vmem, vmem),
        scratch_shapes=[
            pltpu.VMEM((levels, rows, cols), heat.dtype),
            pltpu.VMEM((levels - 1, rows, cols), cond.dtype),
            pltpu.SMEM((levels,), f32),
            pltpu.VMEM((rows, cols), wet.dtype),
            pltpu.VMEM((rows, cols), water.dtype),
            pltpu.VMEM((rows, cols), f32),
            pltpu.VMEM((4, rows + 8, cols + 128), f32),
            pltpu.VMEM((2, 2, 8, cols), f32),
            pltpu.VMEM((2, 2, 8, 128), f32),
            pltpu.VMEM((2, 2, 8, cols), f32),
            pltpu.VMEM((2, 6, 8, 128), f32),
            pltpu.VMEM((n_col, 1, 128), f32),
            pltpu.VMEM((n_row, 1, 128), f32),
            dma((6,)),
            dma((2, 8)),
            dma((2, 8)),
            dma((n_col,)),
            dma((n_col,)),
            dma((n_row,)),
            dma((n_row,)),
        ],
        compiler_params=pltpu.CompilerParams(
            collective_id=0, has_side_effects=True, vmem_limit_bytes=GRANT
        ),
    )(*held)
    return pl.pallas_call(
        finish,
        out_shape=(column, surface),
        in_specs=[vmem, vmem, vmem],
        out_specs=(hbm, hbm),
        scratch_shapes=[pltpu.VMEM((levels, rows, cols), f32), dma((parts + 1,))],
        compiler_params=pltpu.CompilerParams(has_side_effects=True, vmem_limit_bytes=GRANT),
    )(ratios, values, height)


def solution(mesh):
    placed = (
        P(None, "row", "col"),
        P(None, "row", "col"),
        P(),
        P("row", "col"),
        P("row", "col"),
        P("row", "col"),
    )
    return jax.shard_map(
        functools.partial(local, mesh.shape["row"], mesh.shape["col"]),
        mesh=mesh,
        in_specs=placed,
        out_specs=(P(None, "row", "col"), P("row", "col")),
        check_vma=False,
    )
```

time: 18.4 us -> 18.5 us (level)
  no operation moved by 1% of the time
where the time goes in v3:
time: 18.5 us; the launch traced here: 18.3 us
  Pallas kernels  17.7 us (96%)
  between operations  0.64 us (3%)
    pallas_call x1, Pallas kernels, local(): pl.pallas_call(functools.partial(kernel, n_row, n_col), out_shape=(column...  16.5 us
    pallas_call x1, Pallas kernels, local(): pl.pallas_call(finish, out_shape=(column, surface), in_specs=[vmem, vmem,...  1.22 us

profile of v3, /device:TPU:0, one launch (start us, length us, event | category | flops | bytes accessed | tf_op | source)
XLA Modules:
  0.0 18.3 jit_solution(9147238313634449254)
XLA Ops:
  0.6 16.5 %shard_map.77 = (f32[48,32,256]{2,1,0:T(8,128)S(1)}, f32[48,32,256]{2,1,0:T(8,128)S(1)}, f32[32,256]{1,0:T(8,128)S(1)}) custom-call(bf16[48,32,256]{2,1,0:T(8,128)(2,1)} %heat_hbm.1, bf16[47,32,256]{2,1,0:T(8,128)(2,1)} %cond_hbm.1, f32[48]{0:T(128)} %spacing_hbm.1, s32[32,256]{1,0:T(8,128)} %wet_hbm.1, s32[32,256]{1,0:T(8,128)} %water_hbm.1, ...), custom_call_target="tpu_custom_call" | custom-call | tf_op jit(solution)/shard_map/pallas_call | solution.py:406
  17.1 1.2 %shard_map.78 = (f32[48,32,256]{2,1,0:T(8,128)}, f32[32,256]{1,0:T(8,128)}) custom-call(f32[48,32,256]{2,1,0:T(8,128)S(1)} %get-tuple-element.5.ratios, f32[48,32,256]{2,1,0:T(8,128)S(1)} %get-tuple-element.6.values, f32[32,256]{1,0:T(8,128)S(1)} %get-tuple-element.7.height), custom_call_target="tpu_custom_call" | custom-call | tf_op jit(solution)/shard_map/pallas_call | solution.py:437

commit v4 on v3

--- a/solution.py
+++ b/solution.py
@@ -68,15 +68,12 @@
     side,
     land_edge,
     land_side,
-    col_max,
-    row_max,
+    maxima,
     in_sem,
     send_sem,
     recv_sem,
-    col_send,
-    col_recv,
-    row_send,
-    row_recv,
+    max_send,
+    max_recv,
 ):
     levels, rows, cols = heat.shape
     half = cols - 128
@@ -103,20 +100,19 @@
     def greet(r, c):
         pl.semaphore_signal(barrier, inc=1, device_id=(r, c), device_id_type=MESH)
 
-    for off in range(1, n_col):
-        greet(row, lax.rem(col + off, n_col))
-    for off in range(1, n_row):
-        greet(lax.rem(row + off, n_row), col)
-
-    @pl.when(north)
-    def _():
-        greet(up, west)
-        greet(up, east)
-
-    @pl.when(south)
-    def _():
-        greet(down, west)
-        greet(down, east)
+    def peer(i):
+        return lax.rem(row + i // n_col, n_row), lax.rem(col + lax.rem(i, n_col), n_col)
+
+    peers = n_row * n_col
+
+    def for_peers(act):
+        if peers <= 64:
+            for i in range(1, peers):
+                act(jnp.int32(i))
+        else:
+            lax.fori_loop(1, peers, lambda i, none: (act(i), none)[1], None)
+
+    for_peers(lambda i: greet(*peer(i)))
 
     @pl.when(jnp.logical_not(north))
     def _():
@@ -238,8 +234,7 @@
     edge[0, 1] = jnp.where(sub8 >= 4, masked_depth[rows - 8 :], pltpu.roll(mask[rows - 8 :], 4, 0))
     stage_sides(0, (masked_depth, mask))
 
-    diagonal = 2 * (north.astype(jnp.int32) + south.astype(jnp.int32))
-    pl.semaphore_wait(barrier, n_row + n_col - 2 + diagonal)
+    pl.semaphore_wait(barrier, peers - 1)
     start_halo(0)
 
     for get in gets[2:5]:
@@ -275,28 +270,20 @@
     local = bound[:, :128]
     for start in range(128, cols, 128):
         local = jnp.maximum(local, bound[:, start : start + 128])
-    col_max[0] = local
-
-    def tell(buffer, off, sends, recvs, target):
-        return pltpu.make_async_remote_copy(
-            src_ref=buffer.at[0],
-            dst_ref=buffer.at[off],
-            send_sem=sends.at[off],
-            recv_sem=recvs.at[off],
-            device_id=target,
+    maxima[0] = local
+
+    def tell(i):
+        pltpu.make_async_remote_copy(
+            src_ref=maxima.at[0],
+            dst_ref=maxima.at[i],
+            send_sem=max_send,
+            recv_sem=max_recv,
+            device_id=peer(i),
             device_id_type=MESH,
-        )
-
-    col_tells = [
-        tell(col_max, off, col_send, col_recv, (row, lax.rem(col + off, n_col)))
-        for off in range(1, n_col)
-    ]
-    row_tells = [
-        tell(row_max, off, row_send, row_recv, (lax.rem(row + off, n_row), col))
-        for off in range(1, n_row)
-    ]
-    for copy in col_tells:
-        copy.start()
+        ).start()
+
+    for_peers(tell)
+    others = maxima.at[pl.ds(1, peers - 1)]
 
     gets[5].wait()
 
@@ -318,18 +305,7 @@
         return carry
 
     steps = (levels - 1) // GROUP
-    carry = lax.fori_loop(0, steps // 2, forward, (zero, zero, zero))
-
-    for copy in col_tells:
-        copy.wait_recv()
-    best = col_max[0]
-    for off in range(1, n_col):
-        best = jnp.maximum(best, col_max[off])
-    row_max[0] = best
-    for copy in row_tells:
-        copy.start()
-
-    carry = lax.fori_loop(steps // 2, steps, forward, carry)
+    carry = lax.fori_loop(0, steps, forward, (zero, zero, zero))
     for k in range(steps * GROUP, levels):
         coupling = zero
         if k < levels - 1:
@@ -340,12 +316,8 @@
     ext[2, rows:, :cols] = jnp.where(sub8 < 4, land_edge[1, 1], land_edge[1, 0])
     widen_sides(1, 0, 2)
 
-    for copy in row_tells:
-        copy.wait_recv()
-    best = row_max[0]
-    for off in range(1, n_row):
-        best = jnp.maximum(best, row_max[off])
-    top = jnp.max(best, axis=1, keepdims=True)
+    pltpu.make_async_copy(others, others, max_recv).wait()
+    top = jnp.max(jnp.max(maxima[...], axis=0), axis=1, keepdims=True)
 
     theta = 0.5 * (top + SURFACE)
     delta = 0.5 * (top - SURFACE)
@@ -368,8 +340,7 @@
 
     end_halo(0)
     end_halo(1)
-    for copy in col_tells + row_tells:
-        copy.wait_send()
+    pltpu.make_async_copy(others, others, max_send).wait()
 
 
 def finish(ratios, values, height, heat_out, height_out, heat, sem):
@@ -420,15 +391,12 @@
             pltpu.VMEM((2, 2, 8, 128), f32),
             pltpu.VMEM((2, 2, 8, cols), f32),
             pltpu.VMEM((2, 6, 8, 128), f32),
-            pltpu.VMEM((n_col, 1, 128), f32),
-            pltpu.VMEM((n_row, 1, 128), f32),
+            pltpu.VMEM((n_row * n_col, 1, 128), f32),
             dma((6,)),
             dma((2, 8)),
             dma((2, 8)),
-            dma((n_col,)),
-            dma((n_col,)),
-            dma((n_row,)),
-            dma((n_row,)),
+            dma(()),
+            dma(()),
         ],
         compiler_params=pltpu.CompilerParams(
             collective_id=0, has_side_effects=True, vmem_limit_bytes=GRANT

time: 18.5 us -> 16.6 us (0.90)
  Pallas kernels: 17.7 us -> 15.8 us
    pallas_call x1, Pallas kernels: 16.5 us -> 14.6 us  [local(): pl.pallas_call(functools.partial(kernel, n_row, n_col), out_shape=(column...]
where the time goes in v4:
time: 16.6 us; the launch traced here: 16.4 us
  Pallas kernels  15.8 us (95%)
  between operations  0.64 us (4%)
    pallas_call x1, Pallas kernels, local(): pl.pallas_call(functools.partial(kernel, n_row, n_col), out_shape=(column...  14.6 us
    pallas_call x1, Pallas kernels, local(): pl.pallas_call(finish, out_shape=(column, surface), in_specs=[vmem, vmem,...  1.22 us

profile of v4, /device:TPU:0, one launch (start us, length us, event | category | flops | bytes accessed | tf_op | source)
XLA Modules:
  0.0 16.4 jit_solution(1036632921512644399)
XLA Ops:
  0.6 14.6 %shard_map.77 = (f32[48,32,256]{2,1,0:T(8,128)S(1)}, f32[48,32,256]{2,1,0:T(8,128)S(1)}, f32[32,256]{1,0:T(8,128)S(1)}) custom-call(bf16[48,32,256]{2,1,0:T(8,128)(2,1)} %heat_hbm.1, bf16[47,32,256]{2,1,0:T(8,128)(2,1)} %cond_hbm.1, f32[48]{0:T(128)} %spacing_hbm.1, s32[32,256]{1,0:T(8,128)} %wet_hbm.1, s32[32,256]{1,0:T(8,128)} %water_hbm.1, ...), custom_call_target="tpu_custom_call" | custom-call | tf_op jit(solution)/shard_map/pallas_call | solution.py:377
  15.2 1.2 %shard_map.78 = (f32[48,32,256]{2,1,0:T(8,128)}, f32[32,256]{1,0:T(8,128)}) custom-call(f32[48,32,256]{2,1,0:T(8,128)S(1)} %get-tuple-element.5.ratios, f32[48,32,256]{2,1,0:T(8,128)S(1)} %get-tuple-element.6.values, f32[32,256]{1,0:T(8,128)S(1)} %get-tuple-element.7.height), custom_call_target="tpu_custom_call" | custom-call | tf_op jit(solution)/shard_map/pallas_call | solution.py:405

commit v5 on v4

--- a/solution.py
+++ b/solution.py
@@ -116,17 +116,17 @@
 
     @pl.when(jnp.logical_not(north))
     def _():
-        for kind in range(2):
+        for kind in range(1):
             for place in (2, 3):
                 land_side[kind, place] = jnp.zeros((8, 128), jnp.float32)
-            land_edge[kind, 0] = jnp.zeros((8, cols), jnp.float32)
+            land_edge[kind, 0] = jnp.zeros((16, cols), jnp.float32)
 
     @pl.when(jnp.logical_not(south))
     def _():
-        for kind in range(2):
+        for kind in range(1):
             for place in (4, 5):
                 land_side[kind, place] = jnp.zeros((8, 128), jnp.float32)
-            land_edge[kind, 1] = jnp.zeros((8, cols), jnp.float32)
+            land_edge[kind, 1] = jnp.zeros((16, cols), jnp.float32)
 
     def halo_copies(kind):
         def remote(src, dst, slot, target):
@@ -230,13 +230,6 @@
     ext[0, :rows, :cols] = masked_depth
     ext[1, :rows, :cols] = mask
     sub8 = lax.broadcasted_iota(jnp.int32, (8, cols), 0)
-    edge[0, 0] = jnp.where(sub8 < 4, masked_depth[:8], pltpu.roll(mask[:8], 4, 0))
-    edge[0, 1] = jnp.where(sub8 >= 4, masked_depth[rows - 8 :], pltpu.roll(mask[rows - 8 :], 4, 0))
-    stage_sides(0, (masked_depth, mask))
-
-    pl.semaphore_wait(barrier, peers - 1)
-    start_halo(0)
-
     for get in gets[2:5]:
         get.wait()
     wet = wet_ref[...]
@@ -251,13 +244,40 @@
     total = lax.fori_loop(0, levels // GROUP, add_levels, zero)
     forcing = mask * total / math.sqrt(levels)
     ext[2, :rows, :cols] = forcing
-    edge[1, 0] = forcing[:8]
-    edge[1, 1] = forcing[rows - 8 :]
-    stage_sides(1, (forcing,))
-    start_halo(1)
+    edge[0, 0, :8] = jnp.where(sub8 < 4, masked_depth[:8], pltpu.roll(mask[:8], 4, 0))
+    edge[0, 0, 8:] = forcing[:8]
+    edge[0, 1, :8] = jnp.where(
+        sub8 >= 4, masked_depth[rows - 8 :], pltpu.roll(mask[rows - 8 :], 4, 0)
+    )
+    edge[0, 1, 8:] = forcing[rows - 8 :]
+    stage_sides(0, (masked_depth, mask, forcing))
+    pl.semaphore_wait(barrier, peers - 1)
+    start_halo(0)
+
+    gets[5].wait()
+
+    def eliminate(k, carry, coupling):
+        ratio, value, above = carry
+        inverse = 1.0 / (spacing[k] + coupling + above * (1.0 - ratio))
+        source = spacing[k] * heat[k].astype(jnp.float32)
+        ratio = coupling * inverse
+        value = (source + above * value) * inverse
+        ratios[k] = ratio
+        values[k] = value
+        return ratio, value, coupling
+
+    def forward(step, carry):
+        for j in range(GROUP):
+            k = step * GROUP + j
+            coupling = jnp.where(k + 1 < wet_ref[...], cond[k].astype(jnp.float32), 0.0)
+            carry = eliminate(k, carry, coupling)
+        return carry
+
+    steps = (levels - 1) // GROUP
+    carry = lax.fori_loop(0, steps // 2, forward, (zero, zero, zero))
 
     wait_halo(0)
-    from_n, from_s = land_edge[0, 0], land_edge[0, 1]
+    from_n, from_s = land_edge[0, 0, :8], land_edge[0, 1, :8]
     ext[0, rows:, :cols] = jnp.where(sub8 < 4, from_s, from_n)
     ext[1, rows:, :cols] = pltpu.roll(jnp.where(sub8 >= 4, from_s, from_n), 4, 0)
     widen_sides(0, 0, 0)
@@ -285,36 +305,15 @@
     for_peers(tell)
     others = maxima.at[pl.ds(1, peers - 1)]
 
-    gets[5].wait()
-
-    def eliminate(k, carry, coupling):
-        ratio, value, above = carry
-        inverse = 1.0 / (spacing[k] + coupling + above * (1.0 - ratio))
-        source = spacing[k] * heat[k].astype(jnp.float32)
-        ratio = coupling * inverse
-        value = (source + above * value) * inverse
-        ratios[k] = ratio
-        values[k] = value
-        return ratio, value, coupling
-
-    def forward(step, carry):
-        for j in range(GROUP):
-            k = step * GROUP + j
-            coupling = jnp.where(k + 1 < wet_ref[...], cond[k].astype(jnp.float32), 0.0)
-            carry = eliminate(k, carry, coupling)
-        return carry
-
-    steps = (levels - 1) // GROUP
-    carry = lax.fori_loop(0, steps, forward, (zero, zero, zero))
+    carry = lax.fori_loop(steps // 2, steps, forward, carry)
     for k in range(steps * GROUP, levels):
         coupling = zero
         if k < levels - 1:
             coupling = jnp.where(k + 1 < wet_ref[...], cond[k].astype(jnp.float32), 0.0)
         carry = eliminate(k, carry, coupling)
 
-    wait_halo(1)
-    ext[2, rows:, :cols] = jnp.where(sub8 < 4, land_edge[1, 1], land_edge[1, 0])
-    widen_sides(1, 0, 2)
+    ext[2, rows:, :cols] = jnp.where(sub8 < 4, land_edge[0, 1, 8:], land_edge[0, 0, 8:])
+    widen_sides(0, 2, 2)
 
     pltpu.make_async_copy(others, others, max_recv).wait()
     top = jnp.max(jnp.max(maxima[...], axis=0), axis=1, keepdims=True)
@@ -339,7 +338,6 @@
     height_ref[...] = (result + direction)[:rows, :cols]
 
     end_halo(0)
-    end_halo(1)
     pltpu.make_async_copy(others, others, max_send).wait()
 
 
@@ -387,14 +385,14 @@
             pltpu.VMEM((rows, cols), water.dtype),
             pltpu.VMEM((rows, cols), f32),
             pltpu.VMEM((4, rows + 8, cols + 128), f32),
-            pltpu.VMEM((2, 2, 8, cols), f32),
-            pltpu.VMEM((2, 2, 8, 128), f32),
-            pltpu.VMEM((2, 2, 8, cols), f32),
-            pltpu.VMEM((2, 6, 8, 128), f32),
+            pltpu.VMEM((1, 2, 16, cols), f32),
+            pltpu.VMEM((1, 2, 8, 128), f32),
+            pltpu.VMEM((1, 2, 16, cols), f32),
+            pltpu.VMEM((1, 6, 8, 128), f32),
             pltpu.VMEM((n_row * n_col, 1, 128), f32),
             dma((6,)),
-            dma((2, 8)),
-            dma((2, 8)),
+            dma((1, 8)),
+            dma((1, 8)),
             dma(()),
             dma(()),
         ],

time: 16.6 us -> 16.3 us (0.982)
  Pallas kernels: 15.8 us -> 15.6 us
    pallas_call x1, Pallas kernels: 14.6 us -> 14.3 us  [local(): pl.pallas_call(functools.partial(kernel, n_row, n_col), out_shape=(column...]
where the time goes in v5:
time: 16.3 us; the launch traced here: 16.2 us
  Pallas kernels  15.6 us (96%)
  between operations  0.64 us (4%)
    pallas_call x1, Pallas kernels, local(): pl.pallas_call(functools.partial(kernel, n_row, n_col), out_shape=(column...  14.3 us
    pallas_call x1, Pallas kernels, local(): pl.pallas_call(finish, out_shape=(column, surface), in_specs=[vmem, vmem,...  1.22 us

profile of v5, /device:TPU:0, one launch (start us, length us, event | category | flops | bytes accessed | tf_op | source)
XLA Modules:
  0.0 16.2 jit_solution(7593136990942721948)
XLA Ops:
  0.6 14.3 %shard_map.77 = (f32[48,32,256]{2,1,0:T(8,128)S(1)}, f32[48,32,256]{2,1,0:T(8,128)S(1)}, f32[32,256]{1,0:T(8,128)S(1)}) custom-call(bf16[48,32,256]{2,1,0:T(8,128)(2,1)} %heat_hbm.1, bf16[47,32,256]{2,1,0:T(8,128)(2,1)} %cond_hbm.1, f32[48]{0:T(128)} %spacing_hbm.1, s32[32,256]{1,0:T(8,128)} %wet_hbm.1, s32[32,256]{1,0:T(8,128)} %water_hbm.1, ...), custom_call_target="tpu_custom_call" | custom-call | tf_op jit(solution)/shard_map/pallas_call | solution.py:375
  15.0 1.2 %shard_map.78 = (f32[48,32,256]{2,1,0:T(8,128)}, f32[32,256]{1,0:T(8,128)}) custom-call(f32[48,32,256]{2,1,0:T(8,128)S(1)} %get-tuple-element.5.ratios, f32[48,32,256]{2,1,0:T(8,128)S(1)} %get-tuple-element.6.values, f32[32,256]{1,0:T(8,128)S(1)} %get-tuple-element.7.height), custom_call_target="tpu_custom_call" | custom-call | tf_op jit(solution)/shard_map/pallas_call | solution.py:403

commit v6 on v5

--- a/solution.py
+++ b/solution.py
@@ -119,14 +119,14 @@
         for kind in range(1):
             for place in (2, 3):
                 land_side[kind, place] = jnp.zeros((8, 128), jnp.float32)
-            land_edge[kind, 0] = jnp.zeros((16, cols), jnp.float32)
+            land_edge[kind, 0] = jnp.zeros((12, cols), jnp.float32)
 
     @pl.when(jnp.logical_not(south))
     def _():
         for kind in range(1):
             for place in (4, 5):
                 land_side[kind, place] = jnp.zeros((8, 128), jnp.float32)
-            land_edge[kind, 1] = jnp.zeros((16, cols), jnp.float32)
+            land_edge[kind, 1] = jnp.zeros((12, cols), jnp.float32)
 
     def halo_copies(kind):
         def remote(src, dst, slot, target):
@@ -140,15 +140,22 @@
             )
 
         from_west, from_east = side.at[kind, 0], side.at[kind, 1]
+        upper, lower = pl.ds(0, 4), pl.ds(4, 4)
+
+        def corner(src, place, rows_sent, slot, target):
+            return remote(
+                src.at[rows_sent], land_side.at[kind, place, rows_sent], slot, target
+            )
+
         northward = (
             remote(edge.at[kind, 0], land_edge.at[kind, 1], 0, (up, col)),
-            remote(from_west, land_side.at[kind, 5], 1, (up, west)),
-            remote(from_east, land_side.at[kind, 4], 2, (up, east)),
+            corner(from_west, 5, upper, 1, (up, west)),
+            corner(from_east, 4, upper, 2, (up, east)),
         )
         southward = (
             remote(edge.at[kind, 1], land_edge.at[kind, 0], 3, (down, col)),
-            remote(from_west, land_side.at[kind, 3], 4, (down, west)),
-            remote(from_east, land_side.at[kind, 2], 5, (down, east)),
+            corner(from_west, 3, lower, 4, (down, west)),
+            corner(from_east, 2, lower, 5, (down, east)),
         )
         sideways = (
             remote(from_west, land_side.at[kind, 1], 6, (row, west)),
@@ -214,13 +221,15 @@
     lane_c = lax.broadcasted_iota(jnp.int32, (8, 128), 1)
 
     def widen_sides(kind, slot, target):
-        w, e, nw, ne, sw, se = (land_side[kind, place] for place in range(6))
+        w, e = land_side[kind, 0], land_side[kind, 1]
+        a_w = jnp.concatenate([land_side[kind, 4, :4], land_side[kind, 2, 4:]], axis=0)
+        a_e = jnp.concatenate([land_side[kind, 5, :4], land_side[kind, 3, 4:]], axis=0)
         for t in range(tiles):
             by = SLOT * (slot * tiles + t)
             ext[target, pl.ds(8 * t, 8), cols:] = jnp.where(lane_c < 64, shift(e, -by), shift(w, by))
         first, last = SLOT * slot * tiles, SLOT * (slot * tiles + tiles - 1)
-        above = jnp.where(lane_c < 64, shift(ne, -last), shift(nw, last))
-        below = jnp.where(lane_c < 64, shift(se, -first), shift(sw, first))
+        above = jnp.where(lane_c < 64, shift(a_e, -last), shift(a_w, last))
+        below = jnp.where(lane_c < 64, shift(a_e, -first), shift(a_w, first))
         ext[target, rows:, cols:] = jnp.where(sub_c < 4, below, above)
 
     gets[0].wait()
@@ -245,11 +254,11 @@
     forcing = mask * total / math.sqrt(levels)
     ext[2, :rows, :cols] = forcing
     edge[0, 0, :8] = jnp.where(sub8 < 4, masked_depth[:8], pltpu.roll(mask[:8], 4, 0))
-    edge[0, 0, 8:] = forcing[:8]
+    edge[0, 0, 8:] = forcing[:4]
     edge[0, 1, :8] = jnp.where(
         sub8 >= 4, masked_depth[rows - 8 :], pltpu.roll(mask[rows - 8 :], 4, 0)
     )
-    edge[0, 1, 8:] = forcing[rows - 8 :]
+    edge[0, 1, 8:] = forcing[rows - 4 :]
     stage_sides(0, (masked_depth, mask, forcing))
     pl.semaphore_wait(barrier, peers - 1)
     start_halo(0)
@@ -312,8 +321,18 @@
             coupling = jnp.where(k + 1 < wet_ref[...], cond[k].astype(jnp.float32), 0.0)
         carry = eliminate(k, carry, coupling)
 
-    ext[2, rows:, :cols] = jnp.where(sub8 < 4, land_edge[0, 1, 8:], land_edge[0, 0, 8:])
+    ext[2, rows : rows + 4, :cols] = land_edge[0, 1, 8:]
+    ext[2, rows + 4 :, :cols] = land_edge[0, 0, 8:]
     widen_sides(0, 2, 2)
+
+    e, m, residual, centre = ext[0], ext[1], ext[2], ext[3]
+    half_e, half_m = 0.5 * e, 0.5 * m
+
+    def operate(v):
+        return centre * v - (half_e * spread(m * v) + half_m * spread(e * v))
+
+    once = operate(residual)
+    twice = operate(once)
 
     pltpu.make_async_copy(others, others, max_recv).wait()
     top = jnp.max(jnp.max(maxima[...], axis=0), axis=1, keepdims=True)
@@ -321,19 +340,22 @@
     theta = 0.5 * (top + SURFACE)
     delta = 0.5 * (top - SURFACE)
     sigma = theta / delta
-    e, m, residual, centre = ext[0], ext[1], ext[2], ext[3]
-    half_e, half_m = 0.5 * e, 0.5 * m
-    direction = residual * (1.0 / theta)
+    by_theta = 1.0 / theta
+    direction = residual * by_theta
     recur = 1.0 / sigma
     result = jnp.zeros_like(residual)
-    for _ in range(ITERS):
+    for step in range(ITERS):
         result = result + direction
-        image = centre * direction - (
-            half_e * spread(m * direction) + half_m * spread(e * direction)
-        )
+        if step == 0:
+            image = once * by_theta
+        elif step == 1:
+            image = keep * (once * by_theta) + gain * (once - twice * by_theta)
+        else:
+            image = operate(direction)
         residual = residual - image
         recur_next = 1.0 / (2.0 * sigma - recur)
-        direction = (recur_next * recur) * direction + (2.0 * recur_next / delta) * residual
+        keep, gain = recur_next * recur, 2.0 * recur_next / delta
+        direction = keep * direction + gain * residual
         recur = recur_next
     height_ref[...] = (result + direction)[:rows, :cols]
 
@@ -385,9 +407,9 @@
             pltpu.VMEM((rows, cols), water.dtype),
             pltpu.VMEM((rows, cols), f32),
             pltpu.VMEM((4, rows + 8, cols + 128), f32),
-            pltpu.VMEM((1, 2, 16, cols), f32),
+            pltpu.VMEM((1, 2, 12, cols), f32),
             pltpu.VMEM((1, 2, 8, 128), f32),
-            pltpu.VMEM((1, 2, 16, cols), f32),
+            pltpu.VMEM((1, 2, 12, cols), f32),
             pltpu.VMEM((1, 6, 8, 128), f32),
             pltpu.VMEM((n_row * n_col, 1, 128), f32),
             dma((6,)),

time: 16.3 us -> 16 us (0.982)
  Pallas kernels: 15.6 us -> 15.2 us
    pallas_call x1, Pallas kernels: 14.3 us -> 14 us  [local(): pl.pallas_call(functools.partial(kernel, n_row, n_col), out_shape=(column...]
where the time goes in v6:
time: 16 us; the launch traced here: 15.8 us
  Pallas kernels  15.2 us (95%)
  between operations  0.64 us (4%)
    pallas_call x1, Pallas kernels, local(): pl.pallas_call(functools.partial(kernel, n_row, n_col), out_shape=(column...  14 us
    pallas_call x1, Pallas kernels, local(): pl.pallas_call(finish, out_shape=(column, surface), in_specs=[vmem, vmem,...  1.22 us

profile of v6, /device:TPU:0, one launch (start us, length us, event | category | flops | bytes accessed | tf_op | source)
XLA Modules:
  0.0 15.8 jit_solution(5624406658548592442)
XLA Ops:
  0.6 14.0 %shard_map.77 = (f32[48,32,256]{2,1,0:T(8,128)S(1)}, f32[48,32,256]{2,1,0:T(8,128)S(1)}, f32[32,256]{1,0:T(8,128)S(1)}) custom-call(bf16[48,32,256]{2,1,0:T(8,128)(2,1)} %heat_hbm.1, bf16[47,32,256]{2,1,0:T(8,128)(2,1)} %cond_hbm.1, f32[48]{0:T(128)} %spacing_hbm.1, s32[32,256]{1,0:T(8,128)} %wet_hbm.1, s32[32,256]{1,0:T(8,128)} %water_hbm.1, ...), custom_call_target="tpu_custom_call" | custom-call | tf_op jit(solution)/shard_map/pallas_call | solution.py:397
  14.6 1.2 %shard_map.78 = (f32[48,32,256]{2,1,0:T(8,128)}, f32[32,256]{1,0:T(8,128)}) custom-call(f32[48,32,256]{2,1,0:T(8,128)S(1)} %get-tuple-element.5.ratios, f32[48,32,256]{2,1,0:T(8,128)S(1)} %get-tuple-element.6.values, f32[32,256]{1,0:T(8,128)S(1)} %get-tuple-element.7.height), custom_call_target="tpu_custom_call" | custom-call | tf_op jit(solution)/shard_map/pallas_call | solution.py:425

commit v7 on v6

--- a/solution.py
+++ b/solution.py
@@ -116,17 +116,17 @@
 
     @pl.when(jnp.logical_not(north))
     def _():
-        for kind in range(1):
+        for kind in range(2):
             for place in (2, 3):
                 land_side[kind, place] = jnp.zeros((8, 128), jnp.float32)
-            land_edge[kind, 0] = jnp.zeros((12, cols), jnp.float32)
+            land_edge[kind, 0] = jnp.zeros((8, cols), jnp.float32)
 
     @pl.when(jnp.logical_not(south))
     def _():
-        for kind in range(1):
+        for kind in range(2):
             for place in (4, 5):
                 land_side[kind, place] = jnp.zeros((8, 128), jnp.float32)
-            land_edge[kind, 1] = jnp.zeros((12, cols), jnp.float32)
+            land_edge[kind, 1] = jnp.zeros((8, cols), jnp.float32)
 
     def halo_copies(kind):
         def remote(src, dst, slot, target):
@@ -147,13 +147,19 @@
                 src.at[rows_sent], land_side.at[kind, place, rows_sent], slot, target
             )
 
+        def border(own, place, rows_sent, slot, target):
+            if kind == 0:
+                return remote(edge.at[0, own], land_edge.at[0, place], slot, target)
+            src, dst = edge.at[kind, own, rows_sent], land_edge.at[kind, place, rows_sent]
+            return remote(src, dst, slot, target)
+
         northward = (
-            remote(edge.at[kind, 0], land_edge.at[kind, 1], 0, (up, col)),
+            border(0, 1, upper, 0, (up, col)),
             corner(from_west, 5, upper, 1, (up, west)),
             corner(from_east, 4, upper, 2, (up, east)),
         )
         southward = (
-            remote(edge.at[kind, 1], land_edge.at[kind, 0], 3, (down, col)),
+            border(1, 0, lower, 3, (down, col)),
             corner(from_west, 3, lower, 4, (down, west)),
             corner(from_east, 2, lower, 5, (down, east)),
         )
@@ -239,6 +245,12 @@
     ext[0, :rows, :cols] = masked_depth
     ext[1, :rows, :cols] = mask
     sub8 = lax.broadcasted_iota(jnp.int32, (8, cols), 0)
+    edge[0, 0] = jnp.where(sub8 < 4, masked_depth[:8], pltpu.roll(mask[:8], 4, 0))
+    edge[0, 1] = jnp.where(sub8 >= 4, masked_depth[rows - 8 :], pltpu.roll(mask[rows - 8 :], 4, 0))
+    stage_sides(0, (masked_depth, mask))
+    pl.semaphore_wait(barrier, peers - 1)
+    start_halo(0)
+
     for get in gets[2:5]:
         get.wait()
     wet = wet_ref[...]
@@ -253,15 +265,10 @@
     total = lax.fori_loop(0, levels // GROUP, add_levels, zero)
     forcing = mask * total / math.sqrt(levels)
     ext[2, :rows, :cols] = forcing
-    edge[0, 0, :8] = jnp.where(sub8 < 4, masked_depth[:8], pltpu.roll(mask[:8], 4, 0))
-    edge[0, 0, 8:] = forcing[:4]
-    edge[0, 1, :8] = jnp.where(
-        sub8 >= 4, masked_depth[rows - 8 :], pltpu.roll(mask[rows - 8 :], 4, 0)
-    )
-    edge[0, 1, 8:] = forcing[rows - 4 :]
-    stage_sides(0, (masked_depth, mask, forcing))
-    pl.semaphore_wait(barrier, peers - 1)
-    start_halo(0)
+    edge[1, 0] = forcing[:8]
+    edge[1, 1] = forcing[rows - 8 :]
+    stage_sides(1, (forcing,))
+    start_halo(1)
 
     gets[5].wait()
 
@@ -283,10 +290,10 @@
         return carry
 
     steps = (levels - 1) // GROUP
-    carry = lax.fori_loop(0, steps // 2, forward, (zero, zero, zero))
+    carry = lax.fori_loop(0, steps // 4, forward, (zero, zero, zero))
 
     wait_halo(0)
-    from_n, from_s = land_edge[0, 0, :8], land_edge[0, 1, :8]
+    from_n, from_s = land_edge[0, 0], land_edge[0, 1]
     ext[0, rows:, :cols] = jnp.where(sub8 < 4, from_s, from_n)
     ext[1, rows:, :cols] = pltpu.roll(jnp.where(sub8 >= 4, from_s, from_n), 4, 0)
     widen_sides(0, 0, 0)
@@ -314,16 +321,17 @@
     for_peers(tell)
     others = maxima.at[pl.ds(1, peers - 1)]
 
-    carry = lax.fori_loop(steps // 2, steps, forward, carry)
+    carry = lax.fori_loop(steps // 4, steps, forward, carry)
     for k in range(steps * GROUP, levels):
         coupling = zero
         if k < levels - 1:
             coupling = jnp.where(k + 1 < wet_ref[...], cond[k].astype(jnp.float32), 0.0)
         carry = eliminate(k, carry, coupling)
 
-    ext[2, rows : rows + 4, :cols] = land_edge[0, 1, 8:]
-    ext[2, rows + 4 :, :cols] = land_edge[0, 0, 8:]
-    widen_sides(0, 2, 2)
+    wait_halo(1)
+    ext[2, rows : rows + 4, :cols] = land_edge[1, 1, :4]
+    ext[2, rows + 4 :, :cols] = land_edge[1, 0, 4:]
+    widen_sides(1, 0, 2)
 
     e, m, residual, centre = ext[0], ext[1], ext[2], ext[3]
     half_e, half_m = 0.5 * e, 0.5 * m
@@ -360,6 +368,7 @@
     height_ref[...] = (result + direction)[:rows, :cols]
 
     end_halo(0)
+    end_halo(1)
     pltpu.make_async_copy(others, others, max_send).wait()
 
 
@@ -407,14 +416,14 @@
             pltpu.VMEM((rows, cols), water.dtype),
             pltpu.VMEM((rows, cols), f32),
             pltpu.VMEM((4, rows + 8, cols + 128), f32),
-            pltpu.VMEM((1, 2, 12, cols), f32),
-            pltpu.VMEM((1, 2, 8, 128), f32),
-            pltpu.VMEM((1, 2, 12, cols), f32),
-            pltpu.VMEM((1, 6, 8, 128), f32),
+            pltpu.VMEM((2, 2, 8, cols), f32),
+            pltpu.VMEM((2, 2, 8, 128), f32),
+            pltpu.VMEM((2, 2, 8, cols), f32),
+            pltpu.VMEM((2, 6, 8, 128), f32),
             pltpu.VMEM((n_row * n_col, 1, 128), f32),
             dma((6,)),
-            dma((1, 8)),
-            dma((1, 8)),
+            dma((2, 8)),
+            dma((2, 8)),
             dma(()),
             dma(()),
         ],

time: 16 us -> 16 us (level)
  no operation moved by 1% of the time
where the time goes in v7:
time: 16 us; the launch traced here: 15.8 us
  Pallas kernels  15.2 us (95%)
  between operations  0.64 us (4%)
    pallas_call x1, Pallas kernels, local(): pl.pallas_call(functools.partial(kernel, n_row, n_col), out_shape=(column...  14 us
    pallas_call x1, Pallas kernels, local(): pl.pallas_call(finish, out_shape=(column, surface), in_specs=[vmem, vmem,...  1.22 us

profile of v7, /device:TPU:0, one launch (start us, length us, event | category | flops | bytes accessed | tf_op | source)
XLA Modules:
  0.0 15.8 jit_solution(13853238076173803426)
XLA Ops:
  0.6 14.0 %shard_map.77 = (f32[48,32,256]{2,1,0:T(8,128)S(1)}, f32[48,32,256]{2,1,0:T(8,128)S(1)}, f32[32,256]{1,0:T(8,128)S(1)}) custom-call(bf16[48,32,256]{2,1,0:T(8,128)(2,1)} %heat_hbm.1, bf16[47,32,256]{2,1,0:T(8,128)(2,1)} %cond_hbm.1, f32[48]{0:T(128)} %spacing_hbm.1, s32[32,256]{1,0:T(8,128)} %wet_hbm.1, s32[32,256]{1,0:T(8,128)} %water_hbm.1, ...), custom_call_target="tpu_custom_call" | custom-call | tf_op jit(solution)/shard_map/pallas_call | solution.py:406
  14.6 1.2 %shard_map.78 = (f32[48,32,256]{2,1,0:T(8,128)}, f32[32,256]{1,0:T(8,128)}) custom-call(f32[48,32,256]{2,1,0:T(8,128)S(1)} %get-tuple-element.5.ratios, f32[48,32,256]{2,1,0:T(8,128)S(1)} %get-tuple-element.6.values, f32[32,256]{1,0:T(8,128)S(1)} %get-tuple-element.7.height), custom_call_target="tpu_custom_call" | custom-call | tf_op jit(solution)/shard_map/pallas_call | solution.py:434

commit v8 on v6

--- a/solution.py
+++ b/solution.py
@@ -333,7 +333,10 @@
 
     once = operate(residual)
     twice = operate(once)
-
+    thrice = operate(twice)
+
+    end_halo(0)
+    pltpu.make_async_copy(others, others, max_send).wait()
     pltpu.make_async_copy(others, others, max_recv).wait()
     top = jnp.max(jnp.max(maxima[...], axis=0), axis=1, keepdims=True)
 
@@ -347,20 +350,24 @@
     for step in range(ITERS):
         result = result + direction
         if step == 0:
-            image = once * by_theta
+            image, image_2 = once * by_theta, twice * by_theta
+            image_3 = thrice * by_theta
         elif step == 1:
-            image = keep * (once * by_theta) + gain * (once - twice * by_theta)
+            image, image_2 = keep * image + gain * lead, keep * image_2 + gain * lead_2
+        elif step == 2:
+            image = keep * image + gain * lead
         else:
             image = operate(direction)
         residual = residual - image
+        if step == 0:
+            lead, lead_2 = once - image_2, twice - image_3
+        elif step == 1:
+            lead = lead - image_2
         recur_next = 1.0 / (2.0 * sigma - recur)
         keep, gain = recur_next * recur, 2.0 * recur_next / delta
         direction = keep * direction + gain * residual
         recur = recur_next
     height_ref[...] = (result + direction)[:rows, :cols]
-
-    end_halo(0)
-    pltpu.make_async_copy(others, others, max_send).wait()
 
 
 def finish(ratios, values, height, heat_out, height_out, heat, sem):

time: 16 us -> 15.9 us (level)
  no operation moved by 1% of the time
where the time goes in v8:
time: 15.9 us; the launch traced here: 15.7 us
  Pallas kernels  15.1 us (95%)
  between operations  0.64 us (4%)
    pallas_call x1, Pallas kernels, local(): pl.pallas_call(functools.partial(kernel, n_row, n_col), out_shape=(column...  13.9 us
    pallas_call x1, Pallas kernels, local(): pl.pallas_call(finish, out_shape=(column, surface), in_specs=[vmem, vmem,...  1.22 us

profile of v8, /device:TPU:0, one launch (start us, length us, event | category | flops | bytes accessed | tf_op | source)
XLA Modules:
  0.0 15.7 jit_solution(1736295485602511833)
XLA Ops:
  0.6 13.9 %shard_map.77 = (f32[48,32,256]{2,1,0:T(8,128)S(1)}, f32[48,32,256]{2,1,0:T(8,128)S(1)}, f32[32,256]{1,0:T(8,128)S(1)}) custom-call(bf16[48,32,256]{2,1,0:T(8,128)(2,1)} %heat_hbm.1, bf16[47,32,256]{2,1,0:T(8,128)(2,1)} %cond_hbm.1, f32[48]{0:T(128)} %spacing_hbm.1, s32[32,256]{1,0:T(8,128)} %wet_hbm.1, s32[32,256]{1,0:T(8,128)} %water_hbm.1, ...), custom_call_target="tpu_custom_call" | custom-call | tf_op jit(solution)/shard_map/pallas_call | solution.py:404
  14.5 1.2 %shard_map.78 = (f32[48,32,256]{2,1,0:T(8,128)}, f32[32,256]{1,0:T(8,128)}) custom-call(f32[48,32,256]{2,1,0:T(8,128)S(1)} %get-tuple-element.5.ratios, f32[48,32,256]{2,1,0:T(8,128)S(1)} %get-tuple-element.6.values, f32[32,256]{1,0:T(8,128)S(1)} %get-tuple-element.7.height), custom_call_target="tpu_custom_call" | custom-call | tf_op jit(solution)/shard_map/pallas_call | solution.py:432

commit v9 on v8

--- a/solution.py
+++ b/solution.py
@@ -283,7 +283,7 @@
         return carry
 
     steps = (levels - 1) // GROUP
-    carry = lax.fori_loop(0, steps // 2, forward, (zero, zero, zero))
+    carry = lax.fori_loop(0, 3 * steps // 4, forward, (zero, zero, zero))
 
     wait_halo(0)
     from_n, from_s = land_edge[0, 0, :8], land_edge[0, 1, :8]
@@ -314,7 +314,7 @@
     for_peers(tell)
     others = maxima.at[pl.ds(1, peers - 1)]
 
-    carry = lax.fori_loop(steps // 2, steps, forward, carry)
+    carry = lax.fori_loop(3 * steps // 4, steps, forward, carry)
     for k in range(steps * GROUP, levels):
         coupling = zero
         if k < levels - 1:

time: 15.9 us -> 15.9 us (level)
  no operation moved by 1% of the time
where the time goes in v9:
time: 15.9 us; the launch traced here: 15.7 us
  Pallas kernels  15.1 us (95%)
  between operations  0.64 us (4%)
    pallas_call x1, Pallas kernels, local(): pl.pallas_call(functools.partial(kernel, n_row, n_col), out_shape=(column...  13.9 us
    pallas_call x1, Pallas kernels, local(): pl.pallas_call(finish, out_shape=(column, surface), in_specs=[vmem, vmem,...  1.22 us

profile of v9, /device:TPU:0, one launch (start us, length us, event | category | flops | bytes accessed | tf_op | source)
XLA Modules:
  0.0 15.7 jit_solution(31322185326952733)
XLA Ops:
  0.6 13.9 %shard_map.77 = (f32[48,32,256]{2,1,0:T(8,128)S(1)}, f32[48,32,256]{2,1,0:T(8,128)S(1)}, f32[32,256]{1,0:T(8,128)S(1)}) custom-call(bf16[48,32,256]{2,1,0:T(8,128)(2,1)} %heat_hbm.1, bf16[47,32,256]{2,1,0:T(8,128)(2,1)} %cond_hbm.1, f32[48]{0:T(128)} %spacing_hbm.1, s32[32,256]{1,0:T(8,128)} %wet_hbm.1, s32[32,256]{1,0:T(8,128)} %water_hbm.1, ...), custom_call_target="tpu_custom_call" | custom-call | tf_op jit(solution)/shard_map/pallas_call | solution.py:404
  14.5 1.2 %shard_map.78 = (f32[48,32,256]{2,1,0:T(8,128)}, f32[32,256]{1,0:T(8,128)}) custom-call(f32[48,32,256]{2,1,0:T(8,128)S(1)} %get-tuple-element.5.ratios, f32[48,32,256]{2,1,0:T(8,128)S(1)} %get-tuple-element.6.values, f32[32,256]{1,0:T(8,128)S(1)} %get-tuple-element.7.height), custom_call_target="tpu_custom_call" | custom-call | tf_op jit(solution)/shard_map/pallas_call | solution.py:432
